TPU v7x, 32 devices: a whole 2x2x4 slice. The times are simulated.
32 devices in a mesh: expert: 4 (over z), tensor: 8 (over y, x, core).
Axes of the slice: x: 2, y: 2, z: 4, core: 2. Of those that a mesh axis runs over, the one named last changes fastest.
Arguments:
- activations: bfloat16 [3072, 512], P('tensor', 'expert'), may hold values from -6 to 6
- cotangent: bfloat16 [3072, 512], P('tensor', 'expert'), may hold values from -4 to 4
- route_ids: int32 [512, 2], P('expert'), may hold values from 0 to 3, all different within a row; in each aligned block of 128 rows (0 to 127, 128 to 255, ...) at most 80 rows name the same one
- gate_probs: float32 [512, 2], P('expert'), may hold values from 0.2 to 0.8
- gate_weight: bfloat16 [4, 3072, 16384], P('expert', None, 'tensor'), may hold values from -0.15625 to 0.15625
- up_weight: bfloat16 [4, 3072, 16384], P('expert', None, 'tensor'), may hold values from -0.15625 to 0.15625
- down_weight: bfloat16 [4, 16384, 3072], P('expert', 'tensor'), may hold values from -0.046875 to 0.046875
Outputs:
- grad_input: bfloat16 [3072, 512], P('tensor', 'expert')
- score_grad: float32 [512, 2], P('expert')
Inputs may be any that keep to these rules, and one draw needn't show every extreme that they name: `route_ids`: each token names 2 different experts. Among the 128 tokens of one index of the expert axis no expert is named more than 80 times, and in every draw some such block names one expert exactly 80 times.
All inputs are finite; a program needn't handle non-finite values.
Results may differ from a plain program's by a relative error of at most 0.008.
Values may be sent and summed in bfloat16 or wider, within the bound.
A program may use at most 128 MiB of HBM per device.

v0:
```python
import jax
import jax.numpy as jnp
from jax import lax
from jax.sharding import PartitionSpec as P

EXTRA_ROWS = 16


def slot_numbers(route_ids, expert_count, capacity):
    token_count = route_ids.shape[0]
    onehot = route_ids[:, :, None] == jnp.arange(expert_count, dtype=jnp.int32)[None, None, :]
    named = jnp.sum(onehot.astype(jnp.float32), axis=1).astype(jnp.bfloat16)
    order = jnp.arange(token_count, dtype=jnp.int32)
    before = (order[None, :] < order[:, None]).astype(jnp.bfloat16)
    earlier = jnp.dot(before, named, preferred_element_type=jnp.float32)
    position = jnp.sum(jnp.where(onehot, earlier[:, None, :], 0.0), axis=2).astype(jnp.int32)
    return route_ids * capacity + position


def swiglu_backward(gate_sum, up_sum, hidden_grad):
    sigma = jax.nn.sigmoid(gate_sum)
    silu_value = gate_sum * sigma
    grad_up = (hidden_grad * silu_value).astype(jnp.bfloat16)
    grad_gate = (hidden_grad * up_sum * sigma * (1.0 + gate_sum * (1.0 - sigma))).astype(
        jnp.bfloat16
    )
    score_rows = jnp.sum(silu_value * up_sum * hidden_grad, axis=1)
    return (grad_gate, grad_up, score_rows)


def body(activations, cotangent, route_ids, gate_probs, gate_weight, up_weight, down_weight):
    expert_count = lax.axis_size("expert")
    tokens_here = route_ids.shape[0]
    capacity = min(tokens_here, 5 * tokens_here // (2 * expert_count))
    slot_total = expert_count * capacity
    destination = slot_numbers(route_ids, expert_count, capacity)
    slot_range = jnp.arange(slot_total, dtype=jnp.int32)
    matches = destination[:, :, None] == slot_range[None, None, :]
    placing = jnp.sum(matches.astype(jnp.float32), axis=1).astype(jnp.bfloat16)
    weighting = jnp.sum(jnp.where(matches, gate_probs[:, :, None], jnp.float32(0.0)), axis=1)
    gate_local = gate_weight[0]
    up_local = up_weight[0]
    down_local = down_weight[0]
    first_dims = (((0,), (0,)), ((), ()))
    down_dims = (((0,), (1,)), ((), ()))
    hidden_dims = (((1,), (1,)), ((), ()))
    features_here = activations.shape[0]
    send_in = jnp.dot(activations, placing, preferred_element_type=jnp.float32).astype(jnp.bfloat16)
    send_grad = jnp.dot(cotangent, placing, preferred_element_type=jnp.float32).astype(jnp.bfloat16)
    recv_in, recv_grad = (
        lax.all_to_all(send_in, "expert", split_axis=1, concat_axis=1, tiled=True),
        lax.all_to_all(send_grad, "expert", split_axis=1, concat_axis=1, tiled=True),
    )
    feature_piece = lax.all_gather(recv_in, "tensor", axis=0, tiled=True)
    grad_piece = lax.all_gather(recv_grad, "tensor", axis=0, tiled=True)
    gate_rows = gate_local
    up_rows = up_local
    gate_sum = lax.dot_general(
        feature_piece, gate_rows, first_dims, preferred_element_type=jnp.float32
    )
    up_sum = lax.dot_general(feature_piece, up_rows, first_dims, preferred_element_type=jnp.float32)
    hidden_grad = lax.dot_general(
        grad_piece, down_local, down_dims, preferred_element_type=jnp.float32
    )
    gate_sum, up_sum, hidden_grad = (gate_sum, up_sum, hidden_grad)
    grad_gate, grad_up, score_rows = swiglu_backward(gate_sum, up_sum, hidden_grad)
    gate_rows = gate_local
    up_rows = up_local
    term = lax.dot_general(gate_rows, grad_gate, hidden_dims, preferred_element_type=jnp.float32)
    term = term + lax.dot_general(up_rows, grad_up, hidden_dims, preferred_element_type=jnp.float32)
    tensor_count = lax.axis_size("tensor")
    score_high = score_rows.astype(jnp.bfloat16)
    score_low = (score_rows - score_high.astype(jnp.float32)).astype(jnp.bfloat16)
    extra = jnp.concatenate(
        [
            score_high[None, :],
            score_low[None, :],
            jnp.zeros((EXTRA_ROWS - 2, slot_total), jnp.bfloat16),
        ],
        axis=0,
    )
    blocks = term.astype(jnp.bfloat16).reshape(tensor_count, features_here, slot_total)
    extra = jnp.broadcast_to(extra[None], (tensor_count, EXTRA_ROWS, slot_total))
    parts = lax.all_to_all(
        jnp.concatenate([blocks, extra], axis=1), "tensor", split_axis=0, concat_axis=0, tiled=True
    ).astype(jnp.float32)
    totals = jnp.sum(parts, axis=0)
    score = (
        totals[features_here : features_here + 1] + totals[features_here + 1 : features_here + 2]
    )
    score_high = score.astype(jnp.bfloat16)
    score_low = (score - score_high.astype(jnp.float32)).astype(jnp.bfloat16)
    summed = jnp.concatenate(
        [
            totals[:features_here].astype(jnp.bfloat16),
            score_high,
            score_low,
            jnp.zeros((EXTRA_ROWS - 2, slot_total), jnp.bfloat16),
        ],
        axis=0,
    )
    back = lax.all_to_all(summed, "expert", split_axis=1, concat_axis=1, tiled=True)
    back = back.astype(jnp.float32)
    back_terms = back[:features_here]
    back_scores = (
        back[features_here : features_here + 1] + back[features_here + 1 : features_here + 2]
    )
    grad_local = jnp.dot(
        back_terms, weighting.T, precision=lax.Precision.HIGHEST, preferred_element_type=jnp.float32
    )
    score_grad = jnp.sum(
        jnp.where(matches, back_scores[0][None, None, :], jnp.float32(0.0)), axis=2
    )
    grad_input = grad_local.astype(jnp.bfloat16)
    return (grad_input, score_grad)


def solution(mesh):
    in_specs = (
        P("tensor", "expert"),
        P("tensor", "expert"),
        P("expert", None),
        P("expert", None),
        P("expert", None, "tensor"),
        P("expert", None, "tensor"),
        P("expert", "tensor", None),
    )
    out_specs = (P("tensor", "expert"), P("expert", None))
    return jax.shard_map(body, mesh=mesh, in_specs=in_specs, out_specs=out_specs, check_vma=False)
```

profile of v0, /device:TPU:0, one launch (start us, length us, event | category | flops | bytes accessed | tf_op | source)
XLA Modules:
  0.0 178.5 jit_solution(15263084820237573660)
XLA Ops:
  7.2 0.0 copy-start
  7.2 0.0 all-gather.5.cloned.1.call-start
  7.2 0.7 convert_reduce_fusion.2
  7.9 0.1 fusion.23
  8.1 0.7 select_reduce_fusion.2
  8.8 0.7 convert_add_fusion
  9.5 0.2 convolution_convert_fusion
  9.8 14.7 %all_to_all.38 = bf16[384,4,80]{0,2,1:T(8,128)(2,1)} all-to-all(bf16[384,4,80]{0,2,1:T(8,128)(2,1)S(1)} %bitcast.50), channel_id=1, replica_groups=mesh['expert'=4,'tensor'=8] {'expert'}, dimensions={1} | all-to-all | bytes 491520 | tf_op jit(solution)/shard_map/all_to_all | solution.py:51
  24.5 0.0 all-gather.5.cloned.1.call-update
  24.5 0.0 all-gather.3.cloned.1.call-start
  24.6 1.1 convolution_convert_fusion.1
  25.7 10.7 %all_to_all.39 = bf16[384,4,80]{0,2,1:T(8,128)(2,1)} all-to-all(bf16[384,4,80]{0,2,1:T(8,128)(2,1)S(1)} %bitcast.49), channel_id=1, replica_groups=mesh['expert'=4,'tensor'=8] {'expert'}, dimensions={1} | all-to-all | bytes 491520 | tf_op jit(solution)/shard_map/all_to_all | solution.py:52
  36.5 0.0 all-gather.3.cloned.1.call-update
  36.5 14.9 %all-gather.5.cloned.1.call-done = bf16[3072,320]{0,1:T(8,128)(2,1)} async-done(((bf16[384,320]{0,1:T(8,128)(2,1)}), bf16[3072,320]{0,1:T(8,128)(2,1)}) %all-gather.5.cloned.1.call-update) | async-done | bytes 1966096 | tf_op jit(solution)/shard_map/all_gather | solution.py:54
  51.4 9.4 %fusion.2 = f32[320,2048]{1,0:T(8,128)S(1)} fusion(bf16[3072,320]{0,1:T(8,128)(2,1)} %all-gather.5.cloned.1.call-done, bf16[1,3072,2048]{2,1,0:T(8,128)(2,1)} %param.11), kind=kOutput, calls=%fused_computation.2 | convolution fusion | flops 4026531840 | bytes 17170432 | tf_op jit(solution)/shard_map/dot_general | solution.py:58
  60.8 8.8 %fusion.6 = f32[320,2048]{1,0:T(8,128)} fusion(bf16[3072,320]{0,1:T(8,128)(2,1)S(1)} %copy-done.3, bf16[1,3072,2048]{2,1,0:T(8,128)(2,1)} %param.12), kind=kOutput, calls=%fused_computation.6 | convolution fusion | flops 4026531840 | bytes 17170432 | tf_op jit(solution)/shard_map/dot_general | solution.py:61
  69.6 11.3 %all-gather.3.cloned.1.call-done = bf16[3072,320]{0,1:T(8,128)(2,1)} async-done(((bf16[384,320]{0,1:T(8,128)(2,1)}), bf16[3072,320]{0,1:T(8,128)(2,1)}) %all-gather.3.cloned.1.call-update) | async-done | bytes 1966096 | tf_op jit(solution)/shard_map/all_gather | solution.py:55
  80.9 12.0 %multiply_reduce_fusion = (f32[320]{0:T(512)S(1)}, f32[320,2048]{1,0:T(8,128)}) fusion(f32[320,2048]{1,0:T(8,128)} %fusion.6, f32[320,2048]{1,0:T(8,128)S(1)} %fusion.2, bf16[3072,320]{0,1:T(8,128)(2,1)} %all-gather.3.cloned.1.call-done, bf16[1,2048,3072]{2,1,0:T(8,128)(2,1)} %param.13), kind=kOutput, calls=%fused_computation.14 | convolution fusion | flops 4031119104 | bytes 22414592 | tf_op jit(solution)/shard_map/dot_general | solution.py:62
  93.0 12.8 %fusion = f32[320,3072]{1,0:T(8,128)} fusion(bf16[1,3072,2048]{2,1,0:T(8,128)(2,1)} %param.11, f32[320,2048]{1,0:T(8,128)S(1)} %fusion.2, f32[320,2048]{1,0:T(8,128)} %get-tuple-element.7, f32[320,2048]{1,0:T(8,128)} %fusion.6), kind=kOutput, calls=%fused_computation | convolution fusion | flops 4033085440 | bytes 24379392 | tf_op jit(solution)/shard_map/dot_general | solution.py:69
  105.8 12.1 %fusion.16 = bf16[3072,320]{0,1:T(8,128)(2,1)} fusion(f32[320,3072]{1,0:T(8,128)} %fusion, bf16[1,3072,2048]{2,1,0:T(8,128)(2,1)} %param.12, f32[320,2048]{1,0:T(8,128)} %get-tuple-element.7, f32[320,2048]{1,0:T(8,128)S(1)} %fusion.2), kind=kOutput, calls=%fused_computation.13 | convolution fusion | flops 4032430080 | bytes 23724032 | tf_op jit(solution)/shard_map/dot_general | solution.py:70
  117.9 2.9 %copy.40 = bf16[3072,320]{1,0:T(8,128)(2,1)S(1)} copy(bf16[3072,320]{0,1:T(8,128)(2,1)} %fusion.16) | data formatting | bytes 3932160 | tf_op jit(solution)/shard_map/reshape | solution.py:82
  120.9 0.3 pad_maximum_fusion
  121.1 33.0 %all_to_all.40 = bf16[8,400,320]{2,1,0:T(8,128)(2,1)S(1)} all-to-all(bf16[8,400,320]{2,1,0:T(8,128)(2,1)S(1)} %pad_maximum_fusion), channel_id=1, replica_groups=mesh['expert'=4,'tensor'=8] {'tensor'}, dimensions={0} | all-to-all | bytes 4096000 | tf_op jit(solution)/shard_map/all_to_all | solution.py:84
  154.1 0.4 convert_reduce_fusion
  154.5 0.0 copy-start.2
  154.7 0.2 copy.39
  154.8 14.5 %all_to_all.41 = bf16[400,4,80]{0,2,1:T(8,128)(2,1)S(1)} all-to-all(bf16[400,4,80]{0,2,1:T(8,128)(2,1)S(1)} %bitcast.45), channel_id=1, replica_groups=mesh['expert'=4,'tensor'=8] {'expert'}, dimensions={1} | all-to-all | bytes 512000 | tf_op jit(solution)/shard_map/all_to_all | solution.py:102
  169.3 0.1 convert_element_type.115
  169.4 0.2 fusion.22
  169.6 0.1 broadcast_in_dim.57
  169.7 0.7 select_reduce_fusion
  170.4 1.2 convolution_convert_fusion.2
  (16 shorter events, 0.2 us)
Async XLA Ops:
  7.2 2.3 %copy-start = (bf16[384,128]{1,0:T(8,128)(2,1)S(1)}, bf16[384,128]{1,0:T(8,128)(2,1)}, u32[]{:S(2)}) copy-start(bf16[384,128]{1,0:T(8,128)(2,1)} %param.7) | copy-start | bytes 294916
  7.2 44.2 %all-gather.5.cloned.1.call-start = ((), (), s32[]{:S(2)}) async-start(), calls=%async_computation.5 | async-start | bytes 2211840 | tf_op jit(solution)/shard_map/all_gather | solution.py:54
  24.5 56.4 %all-gather.3.cloned.1.call-start = ((), (), s32[]{:S(2)}) async-start(), calls=%async_computation.4 | async-start | bytes 2211840 | tf_op jit(solution)/shard_map/all_gather | solution.py:55
  51.4 9.4 %copy-start.3 = (bf16[3072,320]{0,1:T(8,128)(2,1)S(1)}, bf16[3072,320]{0,1:T(8,128)(2,1)}, u32[]{:S(2)}) copy-start(bf16[3072,320]{0,1:T(8,128)(2,1)} %all-gather.5.cloned.1.call-done) | copy-start | bytes 5898244
  154.1 17.5 %copy-start.1 = (bf16[384,128]{1,0:T(8,128)(2,1)S(1)}, bf16[384,128]{1,0:T(8,128)(2,1)}, u32[]{:S(2)}) copy-start(bf16[384,128]{1,0:T(8,128)(2,1)} %param.7) | copy-start | bytes 294916
  154.5 15.2 %copy-start.2 = (f32[128,2]{0,1:T(2,128)S(1)}, f32[128,2]{0,1:T(2,128)}, u32[]{:S(2)}) copy-start(f32[128,2]{0,1:T(2,128)} %param.10) | copy-start | bytes 3076
Sparse Core Ops, SparseCore 0:
  24.7 26.7 all-gather.4
  53.3 27.6 all-gather.2
where the time goes:
time: 179 us; the launch traced here: 178 us
  blocking collectives  73 us (41%)
  matrix products  57.8 us (32%)
  waiting for transfers between devices  26.3 us (15%)
  between operations  14.2 us (8%)
  other arithmetic  3.87 us (2%)
  local copies, waits for them, and re-layouts  3.26 us (2%)
    all_to_all x1, blocking collectives, body(): lax.all_to_all(jnp.concatenate([blocks, extra], axis=1), 'tensor', split_...  33 us
    all_gather x1, waiting for transfers between devices, body(): feature_piece = lax.all_gather(recv_in, 'tensor', axis=0, tiled=True)  14.9 us
    all_to_all x1, blocking collectives, body(): lax.all_to_all(send_in, 'expert', split_axis=1, concat_axis=1, tiled=True)  14.7 us
    all_to_all x1, blocking collectives, body(): lax.all_to_all(summed, 'expert', split_axis=1, concat_axis=1, tiled=True)  14.5 us
    dot_general x1, matrix products, body(): lax.dot_general(gate_rows, grad_gate, hidden_dims, preferred_element_type...  12.8 us
    dot_general x1, matrix products, body(): lax.dot_general(up_rows, grad_up, hidden_dims, preferred_element_type=jnp...  12.1 us
    dot_general x1, matrix products, body(): lax.dot_general(grad_piece, down_local, down_dims, preferred_element_type...  12 us
    all_gather x1, waiting for transfers between devices, body(): grad_piece = lax.all_gather(recv_grad, 'tensor', axis=0, tiled=True)  11.3 us
  transfers between devices with their start and end apart: 2, of which 2 were waited for; matrix products, arithmetic and copies ran while one was open for 11% of the time, Pallas kernels for 0%

commit v1 on v0

--- a/solution.py
+++ b/solution.py
@@ -51,8 +51,10 @@
         lax.all_to_all(send_in, "expert", split_axis=1, concat_axis=1, tiled=True),
         lax.all_to_all(send_grad, "expert", split_axis=1, concat_axis=1, tiled=True),
     )
-    feature_piece = lax.all_gather(recv_in, "tensor", axis=0, tiled=True)
-    grad_piece = lax.all_gather(recv_grad, "tensor", axis=0, tiled=True)
+    piece_now = lax.all_gather(
+        jnp.concatenate([recv_in, recv_grad], 1), "tensor", axis=0, tiled=True
+    )
+    feature_piece, grad_piece = jnp.split(piece_now, [recv_in.shape[1]], 1)
     gate_rows = gate_local
     up_rows = up_local
     gate_sum = lax.dot_general(

time: 179 us -> 188 us (1.050)
  waiting for transfers between devices: 26.3 us -> 43 us
  blocking collectives: 73 us -> 57.8 us
  starting transfers between devices: 0.08 us -> 6.32 us
    all_to_all x1 -> x0, blocking collectives: 14.7 us -> none  [body(): lax.all_to_all(send_in, 'expert', split_axis=1, concat_axis=1, tiled=True)]
    all_gather x2 -> x1, waiting for transfers between devices: 26.3 us -> 35.5 us  [body(): lax.all_gather(jnp.concatenate([recv_in, recv_grad], 1), 'tensor', axis=0...]
    all_to_all x0 -> x1, waiting for transfers between devices: none -> 7.43 us  [body(): lax.all_to_all(send_in, 'expert', split_axis=1, concat_axis=1, tiled=True)]
    all_to_all x0 -> x1, starting transfers between devices: none -> 6.31 us  [body(): lax.all_to_all(send_in, 'expert', split_axis=1, concat_axis=1, tiled=True)]
  transfers between devices with their start and end apart: 2 -> 2, of which waited for: 2 -> 2; matrix products, arithmetic and copies ran while one was open for 11% -> 1% of each run, Pallas kernels for 0% -> 0%
where the time goes in v1:
time: 188 us; the launch traced here: 187 us
  matrix products  58 us (31%)
  blocking collectives  57.8 us (31%)
  waiting for transfers between devices  43 us (23%)
  between operations  14.2 us (8%)
  starting transfers between devices  6.32 us (3%)
  other arithmetic  4.73 us (3%)
  local copies, waits for them, and re-layouts  3.26 us (2%)
    all_gather x1, waiting for transfers between devices, body(): lax.all_gather(jnp.concatenate([recv_in, recv_grad], 1), 'tensor', axis=0...  35.5 us
    all_to_all x1, blocking collectives, body(): lax.all_to_all(jnp.concatenate([blocks, extra], axis=1), 'tensor', split_...  33 us
    all_to_all x1, blocking collectives, body(): lax.all_to_all(summed, 'expert', split_axis=1, concat_axis=1, tiled=True)  14.5 us
    dot_general x1, matrix products, body(): lax.dot_general(gate_rows, grad_gate, hidden_dims, preferred_element_type...  12.7 us
    dot_general x1, matrix products, body(): lax.dot_general(up_rows, grad_up, hidden_dims, preferred_element_type=jnp...  12.1 us
    dot_general x1, matrix products, body(): lax.dot_general(grad_piece, down_local, down_dims, preferred_element_type...  11.6 us
    all_to_all x1, blocking collectives, body(): lax.all_to_all(send_grad, 'expert', split_axis=1, concat_axis=1, tiled=True)  10.3 us
    dot_general x1, matrix products, body(): lax.dot_general(feature_piece, gate_rows, first_dims, preferred_element_t...  9.42 us
  transfers between devices with their start and end apart: 2, of which 2 were waited for; matrix products, arithmetic and copies ran while one was open for 1% of the time, Pallas kernels for 0%

profile of v1, /device:TPU:0, one launch (start us, length us, event | category | flops | bytes accessed | tf_op | source)
XLA Modules:
  0.0 187.2 jit_solution(7957560003654607083)
XLA Ops:
  7.2 0.0 copy-start
  7.2 0.7 convert_reduce_fusion.2
  7.9 0.1 fusion.26
  8.0 0.7 select_reduce_fusion.2
  8.8 0.7 convert_add_fusion
  9.5 0.0 copy-done
  9.5 0.9 convolution_convert_fusion.1
  10.4 6.3 %all-to-all-start = ((bf16[384,4,80]{0,2,1:T(8,128)(2,1)}), bf16[384,4,80]{0,2,1:T(8,128)(2,1)S(1)}, u32[]{:S(2)}, u32[]{:S(2)}) async-start(bf16[384,4,80]{0,2,1:T(8,128)(2,1)} %bitcast.1), calls=%async_computation | async-start | bytes 491520 | tf_op jit(solution)/shard_map/all_to_all | solution.py:51
  16.7 1.1 convolution_convert_fusion
  17.9 7.4 %all-to-all-done = bf16[384,4,80]{0,2,1:T(8,128)(2,1)S(1)} async-done(((bf16[384,4,80]{0,2,1:T(8,128)(2,1)}), bf16[384,4,80]{0,2,1:T(8,128)(2,1)S(1)}, u32[]{:S(2)}, u32[]{:S(2)}) %all-to-all-start) | async-done | bytes 245792 | tf_op jit(solution)/shard_map/all_to_all | solution.py:51
  25.3 10.3 %all_to_all.38 = bf16[384,4,80]{0,2,1:T(8,128)(2,1)S(1)} all-to-all(bf16[384,4,80]{0,2,1:T(8,128)(2,1)S(1)} %bitcast.43), channel_id=1, replica_groups=mesh['expert'=4,'tensor'=8] {'expert'}, dimensions={1} | all-to-all | bytes 491520 | tf_op jit(solution)/shard_map/all_to_all | solution.py:52
  35.6 0.8 pad_maximum_fusion.1
  36.4 0.0 all-gather.2.cloned.1.call-update
  36.4 35.5 %all-gather.2.cloned.1.call-done = bf16[3072,640]{0,1:T(8,128)(2,1)} async-done(((bf16[384,640]{0,1:T(8,128)(2,1)}), bf16[3072,640]{0,1:T(8,128)(2,1)}) %all-gather.2.cloned.1.call-update) | async-done | bytes 3932176 | tf_op jit(solution)/shard_map/all_gather | solution.py:54
  72.0 9.4 %fusion.2 = f32[320,2048]{1,0:T(8,128)S(1)} fusion(bf16[1,3072,2048]{2,1,0:T(8,128)(2,1)} %param.11, bf16[3072,640]{0,1:T(8,128)(2,1)} %all-gather.2.cloned.1.call-done), kind=kOutput, calls=%fused_computation.2 | convolution fusion | flops 4026531840 | bytes 17170432 | tf_op jit(solution)/shard_map/dot_general | solution.py:60
  81.4 8.8 %fusion.6 = f32[320,2048]{1,0:T(8,128)} fusion(bf16[1,3072,2048]{2,1,0:T(8,128)(2,1)} %param.12, bf16[3072,640]{0,1:T(8,128)(2,1)S(1)} %copy-done.3), kind=kOutput, calls=%fused_computation.6 | convolution fusion | flops 4026531840 | bytes 17170432 | tf_op jit(solution)/shard_map/dot_general | solution.py:63
  90.2 11.6 %multiply_reduce_fusion = (f32[320]{0:T(512)S(1)}, f32[320,2048]{1,0:T(8,128)}) fusion(f32[320,2048]{1,0:T(8,128)} %fusion.6, f32[320,2048]{1,0:T(8,128)S(1)} %fusion.2, bf16[1,2048,3072]{2,1,0:T(8,128)(2,1)} %param.13, bf16[3072,640]{0,1:T(8,128)(2,1)S(1)} %copy-done.3), kind=kOutput, calls=%fused_computation.14 | convolution fusion | flops 4031119104 | bytes 22414592 | tf_op jit(solution)/shard_map/dot_general | solution.py:64
  101.8 12.7 %fusion = f32[320,3072]{1,0:T(8,128)} fusion(bf16[1,3072,2048]{2,1,0:T(8,128)(2,1)} %param.11, f32[320,2048]{1,0:T(8,128)S(1)} %fusion.2, f32[320,2048]{1,0:T(8,128)} %get-tuple-element.7, f32[320,2048]{1,0:T(8,128)} %fusion.6), kind=kOutput, calls=%fused_computation | convolution fusion | flops 4033085440 | bytes 24379392 | tf_op jit(solution)/shard_map/dot_general | solution.py:71
  114.5 12.1 %fusion.16 = bf16[3072,320]{0,1:T(8,128)(2,1)} fusion(f32[320,3072]{1,0:T(8,128)} %fusion, bf16[1,3072,2048]{2,1,0:T(8,128)(2,1)} %param.12, f32[320,2048]{1,0:T(8,128)} %get-tuple-element.7, f32[320,2048]{1,0:T(8,128)S(1)} %fusion.2), kind=kOutput, calls=%fused_computation.13 | convolution fusion | flops 4032430080 | bytes 23724032 | tf_op jit(solution)/shard_map/dot_general | solution.py:72
  126.6 2.9 %copy.40 = bf16[3072,320]{1,0:T(8,128)(2,1)S(1)} copy(bf16[3072,320]{0,1:T(8,128)(2,1)} %fusion.16) | data formatting | bytes 3932160 | tf_op jit(solution)/shard_map/reshape | solution.py:84
  129.6 0.3 pad_maximum_fusion
  129.9 33.0 %all_to_all.39 = bf16[8,400,320]{2,1,0:T(8,128)(2,1)S(1)} all-to-all(bf16[8,400,320]{2,1,0:T(8,128)(2,1)S(1)} %pad_maximum_fusion), channel_id=1, replica_groups=mesh['expert'=4,'tensor'=8] {'tensor'}, dimensions={0} | all-to-all | bytes 4096000 | tf_op jit(solution)/shard_map/all_to_all | solution.py:86
  162.9 0.4 convert_reduce_fusion
  163.3 0.0 copy-start.2
  163.4 0.2 copy.39
  163.6 14.5 %all_to_all.40 = bf16[400,4,80]{0,2,1:T(8,128)(2,1)S(1)} all-to-all(bf16[400,4,80]{0,2,1:T(8,128)(2,1)S(1)} %bitcast.42), channel_id=1, replica_groups=mesh['expert'=4,'tensor'=8] {'expert'}, dimensions={1} | all-to-all | bytes 512000 | tf_op jit(solution)/shard_map/all_to_all | solution.py:104
  178.0 0.1 convert_element_type.115
  178.1 0.2 fusion.25
  178.4 0.1 broadcast_in_dim.57
  178.4 0.0 copy-done.2
  178.4 0.7 select_reduce_fusion
  179.2 1.2 convolution_convert_fusion.2
  (15 shorter events, 0.2 us)
Async XLA Ops:
  7.2 2.3 %copy-start = (bf16[384,128]{1,0:T(8,128)(2,1)S(1)}, bf16[384,128]{1,0:T(8,128)(2,1)}, u32[]{:S(2)}) copy-start(bf16[384,128]{1,0:T(8,128)(2,1)} %param.7) | copy-start | bytes 294916
  10.4 14.9 %all-to-all-start = ((bf16[384,4,80]{0,2,1:T(8,128)(2,1)}), bf16[384,4,80]{0,2,1:T(8,128)(2,1)S(1)}, u32[]{:S(2)}, u32[]{:S(2)}) async-start(bf16[384,4,80]{0,2,1:T(8,128)(2,1)} %bitcast.1), calls=%async_computation | async-start | bytes 491520 | tf_op jit(solution)/shard_map/all_to_all | solution.py:51
  16.7 55.2 %all-gather.2.cloned.1.call-start = ((), (), s32[]{:S(2)}) async-start(), calls=%async_computation.4 | async-start | bytes 4423680 | tf_op jit(solution)/shard_map/all_gather | solution.py:54
  72.0 9.4 %copy-start.3 = (bf16[3072,640]{0,1:T(8,128)(2,1)S(1)}, bf16[3072,640]{0,1:T(8,128)(2,1)}, u32[]{:S(2)}) copy-start(bf16[3072,640]{0,1:T(8,128)(2,1)} %all-gather.2.cloned.1.call-done) | copy-start | bytes 11796484
  162.9 17.5 %copy-start.1 = (bf16[384,128]{1,0:T(8,128)(2,1)S(1)}, bf16[384,128]{1,0:T(8,128)(2,1)}, u32[]{:S(2)}) copy-start(bf16[384,128]{1,0:T(8,128)(2,1)} %param.7) | copy-start | bytes 294916
  163.3 15.2 %copy-start.2 = (f32[128,2]{0,1:T(2,128)S(1)}, f32[128,2]{0,1:T(2,128)}, u32[]{:S(2)}) copy-start(f32[128,2]{0,1:T(2,128)} %param.10) | copy-start | bytes 3076
Sparse Core Ops, SparseCore 0:
  36.6 35.3 all-gather.1
